TPU v7x, 32 devices: a whole 2x2x4 slice. The times are simulated.
32 devices in a mesh: groups: 2 (over y), sec: 4 (over z), blk: 4 (over x, core).
Axes of the slice: x: 2, y: 2, z: 4, core: 2. Of those that a mesh axis runs over, the one named last changes fastest.
Arguments:
- psi: bfloat16 [8, 4, 256, 256], P(('groups', 'sec'), 'blk'), parts along dimension 0, may hold values from -6 to 6
- own_env: bfloat16 [8, 4, 17, 256, 256], P(('groups', 'sec'), 'blk'), parts along dimension 0, may hold values from -0.375 to 0.375
- handoff_env: bfloat16 [8, 4, 17, 256, 256], P(('groups', 'sec'), 'blk'), parts along dimension 0, may hold values from -0.375 to 0.375
- sources: int32 [8, 4, 17], P(('groups', 'sec'), 'blk'), parts along dimension 0, may hold values from 0 to 3, as said below
Outputs:
- applied: bfloat16 [8, 4, 256, 256], P(('groups', 'sec'), 'blk'), parts along dimension 0
- rayleigh: float32 [8], P(('groups', 'sec')), parts along dimension 0
- residual_scale: float32 [8], P(('groups', 'sec')), parts along dimension 0
There are 2 independent parts, one for each index of `groups`. A program takes and returns all parts, laid end to end along the dimension named above; each array names one. Nothing has to cross between parts.
Inputs may be any that keep to these rules, and one draw needn't show every extreme that they name: `sources`: every entry names a sector of the same section, and the 17 channels of each output sector name every one of the 4 sectors of its section.
All inputs are finite; a program needn't handle non-finite values.
Results may differ from a plain program's by a relative error of at most 0.0064.
Values may be sent and summed in bfloat16 or wider, within the bound.
A program may use at most 64 MiB of HBM per device.

v0:
```python
import jax
import jax.numpy as jnp
from jax import lax
from jax.sharding import PartitionSpec as P


def from_partner(value, axis, apart):
    return lax.ppermute(value, axis, [(i, i ^ 1 << apart) for i in range(lax.axis_size(axis))])


def contract(picked, left, right):
    inner = jnp.einsum("qcab,qcbd->qcad", picked, right, preferred_element_type=jnp.float32).astype(
        jnp.bfloat16
    )
    return jnp.einsum("qcab,qcbd->qad", left, inner, preferred_element_type=jnp.float32)


def shards(psi, own_env, handoff_env, sources):
    partner = from_partner(handoff_env, "sec", 0)
    even = lax.axis_index("sec") % 2 == 0
    left = jnp.where(even, own_env[0], partner[0])
    right = jnp.where(even, partner[0], own_env[0])
    sec_dev = psi.shape[1]
    channels = sources.shape[2]
    block = psi.shape[2]
    width = lax.axis_size("blk")
    own_list = sources[0].reshape(-1)
    vector = psi[0]
    whole_psi = lax.all_gather(vector, "blk", axis=0, tiled=True)
    picked = whole_psi[own_list].reshape(sec_dev, channels, block, block)
    first = contract(picked, left, right)
    widened = vector.astype(jnp.float32)
    count = width * sec_dev * block * block
    along, mass, squared = lax.psum(
        (jnp.sum(widened * first), jnp.sum(widened * widened), jnp.sum(first * first)), "blk"
    )
    alpha = along / mass
    resid = first - alpha * widened
    power = squared - alpha * along
    scale = jnp.sqrt(power / count + 1e-06)
    second = (resid / scale).astype(jnp.bfloat16)
    whole_second = lax.all_gather(second, "blk", axis=0, tiled=True)
    repicked = whole_second[own_list].reshape(sec_dev, channels, block, block)
    applied = contract(repicked, left, right).astype(jnp.bfloat16)
    return (applied[None], alpha.reshape(1), scale.reshape(1))


def solution(mesh):
    in_specs = (
        P(("groups", "sec"), "blk", None, None),
        P(("groups", "sec"), "blk", None, None, None),
        P(("groups", "sec"), "blk", None, None, None),
        P(("groups", "sec"), "blk", None),
    )
    out_specs = (
        P(("groups", "sec"), "blk", None, None),
        P(("groups", "sec")),
        P(("groups", "sec")),
    )
    return jax.shard_map(shards, mesh=mesh, in_specs=in_specs, out_specs=out_specs, check_vma=False)
```

profile of v0, /device:TPU:1, one launch (start us, length us, event | category | flops | bytes accessed | tf_op | source)
XLA Modules:
  0.0 80.8 jit_solution(6384535929502615253)
XLA Ops:
  0.6 2.2 %collective-permute-start = (bf16[1,1,17,256,256]{4,3,2,1,0:T(8,128)(2,1)}, bf16[1,1,17,256,256]{4,3,2,1,0:T(8,128)(2,1)}, u32[]{:S(2)}, u32[]{:S(2)}) collective-permute-start(bf16[1,1,17,256,256]{4,3,2,1,0:T(8,128)(2,1)} %param.6), channel_id=1, source_target_pairs={{0,4},{4,0},{8,12},{12,8},{1,5},{5,1},{9,13},{13,9},{2,6},{6,2},{1... | collective-permute-start | bytes 6684680 | tf_op jit(solution)/shard_map/ppermute | solution.py:8
  2.8 0.7 fusion.53
  3.5 8.2 %all-gather = bf16[4,1,256,256]{3,2,1,0:T(8,128)(2,1)S(1)} all-gather(bf16[1,1,256,256]{3,2,1,0:T(8,128)(2,1)} %param.4), channel_id=2, replica_groups=mesh['groups'=2,'sec'=4,'blk'=4] {'blk'}, dimensions={0}, use_global_device_ids=true | all-gather | bytes 655360 | tf_op jit(solution)/shard_map/all_gather | solution.py:29
  11.6 0.0 copy-start
  11.7 0.7 gather_fusion
  12.3 0.2 copy-done
  12.6 0.7 fusion.52
  13.2 38.1 %collective-permute-done = bf16[1,1,17,256,256]{4,3,2,1,0:T(8,128)(2,1)} collective-permute-done((bf16[1,1,17,256,256]{4,3,2,1,0:T(8,128)(2,1)}, bf16[1,1,17,256,256]{4,3,2,1,0:T(8,128)(2,1)}, u32[]{:S(2)}, u32[]{:S(2)}) %collective-permute-start) | collective-permute-done | bytes 2228256 | tf_op jit(solution)/shard_map/ppermute | solution.py:8
  51.3 4.4 %fusion.48 = (f32[]{:T(128)}, f32[]{:T(128)}, f32[256,256]{1,0:T(8,128)S(1)}) fusion(bf16[1,1,256,256]{3,2,1,0:T(8,128)(2,1)S(1)} %copy-done, bf16[17,256,256]{2,1,0:T(8,128)(2,1)S(1)} %gather_fusion, bf16[1,1,17,256,256]{4,3,2,1,0:T(8,128)(2,1)} %collective-permute-done, bf16[1,1,17,256,256]{4,3,2,1,0:T(8,128)(2,1)} %param.5, pred[]{:T(512)S(6)} %eq.5), kind=kOutput, calls=%fused_computation.22 | convolution fusion | flops 1144520704 | bytes 7077897 | tf_op jit(solution)/shard_map/qcab,qcbd->qad/dot_general | solution.py:15
  55.7 6.9 %all-reduce = (f32[]{:T(128)}, f32[]{:T(128)}, f32[]{:T(128)}) all-reduce(f32[]{:T(128)} %get-tuple-element.4, f32[]{:T(128)} %get-tuple-element.3, f32[]{:T(128)} %fusion.52), channel_id=1, replica_groups=mesh['groups'=2,'sec'=4,'blk'=4] {'blk'}, use_global_device_ids=true, to_apply=%region_5.6 | all-reduce | flops 3 | bytes 24 | tf_op jit(solution)/shard_map/psum | solution.py:34
  65.4 7.9 %all-gather.1 = bf16[1024,256]{1,0:T(8,128)(2,1)S(1)} all-gather(bf16[256,256]{1,0:T(8,128)(2,1)S(1)} %fusion.51), channel_id=3, replica_groups=mesh['groups'=2,'sec'=4,'blk'=4] {'blk'}, dimensions={0}, use_global_device_ids=true | all-gather | bytes 655360 | tf_op jit(solution)/shard_map/all_gather | solution.py:42
  73.3 0.7 gather_fusion.1
  74.0 4.5 %fusion.39 = bf16[1,1,256,256]{3,2,1,0:T(8,128)(2,1)} fusion(bf16[17,256,256]{2,1,0:T(8,128)(2,1)S(1)} %gather_fusion.1, bf16[1,1,17,256,256]{4,3,2,1,0:T(8,128)(2,1)} %param.5, bf16[1,1,17,256,256]{4,3,2,1,0:T(8,128)(2,1)} %collective-permute-done, pred[]{:T(512)S(6)} %eq.5), kind=kOutput, calls=%fused_computation.17 | convolution fusion | flops 1144258560 | bytes 6815745 | tf_op jit(solution)/shard_map/qcab,qcbd->qad/dot_general | solution.py:15
  (2 shorter events, 0.1 us)
Async XLA Ops:
  0.6 50.7 %collective-permute-start = (bf16[1,1,17,256,256]{4,3,2,1,0:T(8,128)(2,1)}, bf16[1,1,17,256,256]{4,3,2,1,0:T(8,128)(2,1)}, u32[]{:S(2)}, u32[]{:S(2)}) collective-permute-start(bf16[1,1,17,256,256]{4,3,2,1,0:T(8,128)(2,1)} %param.6), channel_id=1, source_target_pairs={{0,4},{4,0},{8,12},{12,8},{1,5},{5,1},{9,13},{13,9},{2,6},{6,2},{1... | collective-permute-start | bytes 6684680 | tf_op jit(solution)/shard_map/ppermute | solution.py:8
  11.6 0.9 %copy-start = (bf16[1,1,256,256]{3,2,1,0:T(8,128)(2,1)S(1)}, bf16[1,1,256,256]{3,2,1,0:T(8,128)(2,1)}, u32[]{:S(2)}) copy-start(bf16[1,1,256,256]{3,2,1,0:T(8,128)(2,1)} %param.4) | copy-start | bytes 393220
where the time goes:
time: 81.1 us; the launch traced here: 80.8 us
  waiting for transfers between devices  38.1 us (47%)
  blocking collectives  23 us (28%)
  matrix products  8.91 us (11%)
  between operations  5.62 us (7%)
  starting transfers between devices  2.19 us (3%)
  local copies, waits for them, and re-layouts  1.59 us (2%)
  other arithmetic  1.38 us (2%)
    ppermute x1, waiting for transfers between devices, from_partner(): lax.ppermute(value, axis, [(i, i ^ 1 << apart) for i in range(lax.axis_si...  38.1 us
    dot_general x2, matrix products, contract(): jnp.einsum('qcab,qcbd->qad', left, inner, preferred_element_type=jnp.floa...  8.91 us
    all_gather x1, blocking collectives, shards(): whole_psi = lax.all_gather(vector, 'blk', axis=0, tiled=True)  8.16 us
    all_gather x1, blocking collectives, shards(): whole_second = lax.all_gather(second, 'blk', axis=0, tiled=True)  7.9 us
    psum x1, blocking collectives, shards(): lax.psum((jnp.sum(widened * first), jnp.sum(widened * widened), jnp.sum(f...  6.94 us
    ppermute x1, starting transfers between devices, from_partner(): lax.ppermute(value, axis, [(i, i ^ 1 << apart) for i in range(lax.axis_si...  2.19 us
  transfers between devices with their start and end apart: 1, of which 1 were waited for; matrix products, arithmetic and copies ran while one was open for 2% of the time, Pallas kernels for 0%

commit v1 on v0

v1 whole, which is shorter than its diff:
```python
import functools

import jax
import jax.numpy as jnp
from jax import lax
from jax.experimental import pallas as pl
from jax.experimental.pallas import tpu as pltpu
from jax.sharding import PartitionSpec as P

MESH = pl.DeviceIdType.MESH


def kernel(
    width, pieces,
    psi_hbm, own_hbm, hand_hbm, src_ref,
    out_ref, alpha_ref, scale_ref,
    env, whole, whole2, first_ref, stats,
    load_sem, z_send, z_recv, psi_send, psi_recv, stat_send, stat_recv,
    v_send, v_recv, f_send, f_recv,
):
    channels = own_hbm.shape[2]
    block = psi_hbm.shape[2]
    sec = lax.axis_index("sec")
    me = lax.axis_index("blk")
    odd = lax.rem(sec, 2)
    partner = {"sec": sec + 1 - 2 * odd}
    core = lax.rem(me, 2)
    sibling = me + 1 - 2 * core
    peers = [lax.rem(me + k, width) for k in range(1, width)]
    across = [lax.rem(me + 2 * k, width) for k in range(1, width // 2)]
    behind = [lax.rem(me + width - 2 * k, width) for k in range(1, width // 2)]
    sib_behind = [lax.rem(sibling + width - 2 * k, width) for k in range(1, width // 2)]

    barrier = pltpu.get_barrier_semaphore()
    pl.semaphore_signal(barrier, inc=1, device_id=partner, device_id_type=MESH)
    for k in peers:
        pl.semaphore_signal(barrier, inc=1, device_id={"blk": k}, device_id_type=MESH)
    load_own = pltpu.make_async_copy(own_hbm.at[0, 0], env.at[0], load_sem.at[0])
    load_psi = pltpu.make_async_copy(psi_hbm.at[0, 0], whole.at[me], load_sem.at[1])
    load_own.start()
    load_psi.start()
    pl.semaphore_wait(barrier, width)

    def z_copy(c):
        return pltpu.make_async_remote_copy(
            src_ref=hand_hbm.at[0, 0, c], dst_ref=env.at[1, c],
            send_sem=z_send.at[c], recv_sem=z_recv.at[c],
            device_id=partner, device_id_type=MESH,
        )

    @pl.loop(0, channels)
    def _(c):
        z_copy(c).start()

    def psi_copy(k):
        return pltpu.make_async_remote_copy(
            src_ref=psi_hbm.at[0, 0], dst_ref=whole.at[me],
            send_sem=psi_send.at[k], recv_sem=psi_recv.at[k],
            device_id={"blk": peers[k]}, device_id_type=MESH,
        )

    for k in range(width - 1):
        psi_copy(k).start()
    load_own.wait()
    load_psi.wait()
    for k in range(width - 1):
        psi_copy(k).wait()

    first_ref[...] = jnp.zeros_like(first_ref)

    def term(v, c):
        inner = jnp.dot(
            v[src_ref[0, 0, c]], env[1 - odd, c], preferred_element_type=jnp.float32
        ).astype(jnp.bfloat16)
        return jnp.dot(env[odd, c], inner, preferred_element_type=jnp.float32)

    @pl.loop(0, channels)
    def _(c):
        z_copy(c).wait_recv()
        first_ref[...] += term(whole, c)

    p = whole[me].astype(jnp.float32)
    f = first_ref[...]
    along = jnp.sum(p * f, keepdims=True)
    mass = jnp.sum(p * p, keepdims=True)
    own_alpha = jnp.where(mass > 0, along / jnp.where(mass > 0, mass, 1.0), 0.0)
    rest = f - own_alpha * p
    beside = jnp.sum(rest * rest, keepdims=True)
    row = lax.broadcasted_iota(jnp.int32, (8, 128), 0)
    stats[me] = jnp.where(row == 0, along, jnp.where(row == 1, mass, beside))

    def stat_copy(k):
        return pltpu.make_async_remote_copy(
            src_ref=stats.at[me], dst_ref=stats.at[me],
            send_sem=stat_send.at[k], recv_sem=stat_recv.at[k],
            device_id={"blk": peers[k]}, device_id_type=MESH,
        )

    for k in range(width - 1):
        stat_copy(k).start()
    for k in range(width - 1):
        stat_copy(k).wait()
    tiles = [stats[j] for j in range(width)]
    along_all = sum(t[0:1, 0:1] for t in tiles)
    mass_all = sum(t[1:2, 0:1] for t in tiles)
    alpha = along_all / mass_all
    power = jnp.zeros_like(alpha)
    for t in tiles:
        a, m, r = t[0:1, 0:1], t[1:2, 0:1], t[2:3, 0:1]
        off = jnp.where(m > 0, a / jnp.where(m > 0, m, 1.0), 0.0) - alpha
        power += r + off * off * m
    scale = jnp.sqrt(power / (width * block * block) + 1e-06)
    whole2[me] = ((f - alpha * p) / scale).astype(jnp.bfloat16)

    rows = block // pieces

    def v_copy(k, i):
        target = sibling if k < 0 else across[k]
        part = whole2.at[me, pl.ds(i * rows, rows)]
        return pltpu.make_async_remote_copy(
            src_ref=part, dst_ref=part,
            send_sem=v_send.at[k + 1, i], recv_sem=v_recv.at[k + 1, i],
            device_id={"blk": target}, device_id_type=MESH,
        )

    def f_copy(k, i):
        part = whole2.at[behind[k], pl.ds(i * rows, rows)]
        return pltpu.make_async_remote_copy(
            src_ref=part, dst_ref=part,
            send_sem=f_send.at[k, i], recv_sem=f_recv.at[k, i],
            device_id={"blk": sibling}, device_id_type=MESH,
        )

    hops = width // 2 - 1
    for k in range(hops):
        for i in range(pieces):
            v_copy(k, i).start()
    for i in range(pieces):
        v_copy(-1, i).start()
    for k in range(hops):
        for i in range(pieces):
            v_copy(k, i).wait_recv()
            f_copy(k, i).start()
    for i in range(pieces):
        v_copy(-1, i).wait_recv()
    for k in range(hops):
        for i in range(pieces):
            f_copy(k, i).wait_recv()

    total = term(whole2, 0)
    for c in range(1, channels):
        total += term(whole2, c)
    out_ref[0, 0] = total.astype(jnp.bfloat16)
    alpha_ref[0] = alpha[0, 0]
    scale_ref[0] = scale[0, 0]

    for k in range(-1, hops):
        for i in range(pieces):
            v_copy(k, i).wait_send()
    for k in range(hops):
        for i in range(pieces):
            f_copy(k, i).wait_send()

    @pl.loop(0, channels)
    def _(c):
        z_copy(c).wait_send()


def shards(width, psi, own_env, handoff_env, sources):
    channels = sources.shape[2]
    block = psi.shape[2]
    pieces = 2
    hops = width // 2 - 1
    dma = pltpu.SemaphoreType.DMA
    bf16, f32 = jnp.bfloat16, jnp.float32
    hbm = pl.BlockSpec(memory_space=pl.ANY)
    return pl.pallas_call(
        functools.partial(kernel, width, pieces),
        out_shape=(
            jax.ShapeDtypeStruct(psi.shape, bf16),
            jax.ShapeDtypeStruct((1,), f32),
            jax.ShapeDtypeStruct((1,), f32),
        ),
        in_specs=[hbm, hbm, hbm, pl.BlockSpec(memory_space=pltpu.SMEM)],
        out_specs=(
            pl.BlockSpec(memory_space=pltpu.VMEM),
            pl.BlockSpec(memory_space=pltpu.SMEM),
            pl.BlockSpec(memory_space=pltpu.SMEM),
        ),
        scratch_shapes=[
            pltpu.VMEM((2, channels, block, block), bf16),
            pltpu.VMEM((width, block, block), bf16),
            pltpu.VMEM((width, block, block), bf16),
            pltpu.VMEM((block, block), f32),
            pltpu.VMEM((width, 8, 128), f32),
            dma((2,)),
            dma((channels,)), dma((channels,)),
            dma((width - 1,)), dma((width - 1,)),
            dma((width - 1,)), dma((width - 1,)),
            dma((hops + 1, pieces)), dma((hops + 1, pieces)),
            dma((hops, pieces)), dma((hops, pieces)),
        ],
        compiler_params=pltpu.CompilerParams(
            collective_id=0, has_side_effects=True, vmem_limit_bytes=40 * 2**20
        ),
        cost_estimate=pl.CostEstimate(
            flops=8 * channels * block**3, bytes_accessed=6 * channels * block**2,
            transcendentals=0,
        ),
    )(psi, own_env, handoff_env, sources)


def solution(mesh):
    in_specs = (
        P(("groups", "sec"), "blk", None, None),
        P(("groups", "sec"), "blk", None, None, None),
        P(("groups", "sec"), "blk", None, None, None),
        P(("groups", "sec"), "blk", None),
    )
    out_specs = (
        P(("groups", "sec"), "blk", None, None),
        P(("groups", "sec")),
        P(("groups", "sec")),
    )
    body = functools.partial(shards, mesh.shape["blk"])
    return jax.shard_map(body, mesh=mesh, in_specs=in_specs, out_specs=out_specs, check_vma=False)
```

time: 81.1 us -> 75.4 us (0.930)
  Pallas kernels: 0 us -> 65.7 us
  waiting for transfers between devices: 38.1 us -> 0 us
  blocking collectives: 23 us -> 0 us
  matrix products: 8.91 us -> 0 us
  local copies, waits for them, and re-layouts: 1.59 us -> 5.46 us
  starting transfers between devices: 2.19 us -> 0 us
  between operations: 5.62 us -> 4.08 us
  other arithmetic: 1.38 us -> 0 us
    pallas_call x0 -> x1, Pallas kernels: none -> 65.7 us  [shards(): pl.pallas_call(functools.partial(kernel, width, pieces), out_shape=(jax.S...]
    ppermute x1 -> x0, waiting for transfers between devices: 38.1 us -> none  [from_partner(): lax.ppermute(value, axis, [(i, i ^ 1 << apart) for i in range(lax.axis_si...]
    all_gather x2 -> x0, blocking collectives: 16.1 us -> none  [the longest x1 8.16 us: shards(): whole_psi = lax.all_gather(vector, 'blk', axis=0, tiled=True)]
    dot_general x2 -> x0, matrix products: 8.91 us -> none  [contract(): jnp.einsum('qcab,qcbd->qad', left, inner, preferred_element_type=jnp.floa...]
    psum x1 -> x0, blocking collectives: 6.94 us -> none  [shards(): lax.psum((jnp.sum(widened * first), jnp.sum(widened * widened), jnp.sum(f...]
    unnamed x2 -> x9, local copies, waits for them, and re-layouts: 0.21 us -> 5.46 us
    ppermute x1 -> x0, starting transfers between devices: 2.19 us -> none  [from_partner(): lax.ppermute(value, axis, [(i, i ^ 1 << apart) for i in range(lax.axis_si...]
    gather x2 -> x0, local copies, waits for them, and re-layouts: 1.38 us -> none  [the longest x1 0.69 us: shards(): picked = whole_psi[own_list].reshape(sec_dev, channels, block, block)]
  transfers between devices with their start and end apart: 1 -> 0, of which waited for: 1 -> 0; matrix products, arithmetic and copies ran while one was open for 2% -> 0% of each run, Pallas kernels for 0% -> 0%
where the time goes in v1:
time: 75.4 us; the launch traced here: 75.2 us
  Pallas kernels  65.7 us (87%)
  local copies, waits for them, and re-layouts  5.46 us (7%)
  between operations  4.08 us (5%)
    pallas_call x1, Pallas kernels, shards(): pl.pallas_call(functools.partial(kernel, width, pieces), out_shape=(jax.S...  65.7 us
    unnamed x9, local copies, waits for them, and re-layouts  5.46 us

profile of v1, /device:TPU:1, one launch (start us, length us, event | category | flops | bytes accessed | tf_op | source)
XLA Modules:
  0.0 75.2 jit_solution(6962345522912299257)
XLA Ops:
  0.6 0.0 copy-start
  0.6 1.6 %copy-done = bf16[1,1,17,256,256]{4,3,2,1,0:T(8,128)(2,1)S(1)} copy-done((bf16[1,1,17,256,256]{4,3,2,1,0:T(8,128)(2,1)S(1)}, bf16[1,1,17,256,256]{4,3,2,1,0:T(8,128)(2,1)}, u32[]{:S(2)}) %copy-start) | copy-done | bytes 2228248
  2.3 0.0 copy-start.1
  2.3 1.6 %copy-done.1 = bf16[1,1,17,256,256]{4,3,2,1,0:T(8,128)(2,1)S(1)} copy-done((bf16[1,1,17,256,256]{4,3,2,1,0:T(8,128)(2,1)S(1)}, bf16[1,1,17,256,256]{4,3,2,1,0:T(8,128)(2,1)}, u32[]{:S(2)}) %copy-start.1) | copy-done | bytes 2228248
  3.9 0.0 copy-start.2
  3.9 0.9 %copy-done.2 = bf16[1,1,256,256]{3,2,1,0:T(8,128)(2,1)S(1)} copy-done((bf16[1,1,256,256]{3,2,1,0:T(8,128)(2,1)S(1)}, bf16[1,1,256,256]{3,2,1,0:T(8,128)(2,1)}, u32[]{:S(2)}) %copy-start.2) | copy-done | bytes 131096
  4.8 0.0 copy-start.3
  4.8 0.7 copy-done.3
  5.4 65.7 %shard_map.67 = (bf16[1,1,256,256]{3,2,1,0:T(8,128)(2,1)S(1)}, f32[1]{0:T(128)}, f32[1]{0:T(128)}) custom-call(bf16[1,1,256,256]{3,2,1,0:T(8,128)(2,1)S(1)} %copy-done.2, bf16[1,1,17,256,256]{4,3,2,1,0:T(8,128)(2,1)S(1)} %copy-done, bf16[1,1,17,256,256]{4,3,2,1,0:T(8,128)(2,1)S(1)} %copy-done.1, s32[1,1,17]{2,1,0:T(1,128)S(1)} %copy-done.3), custom_call_target="tpu_custom_call" | custom-call | flops 2281701376 | bytes 6684672 | tf_op jit(solution)/shard_map/pallas_call | solution.py:177
  71.1 0.7 copy.10
Async XLA Ops:
  0.6 1.6 %copy-start = (bf16[1,1,17,256,256]{4,3,2,1,0:T(8,128)(2,1)S(1)}, bf16[1,1,17,256,256]{4,3,2,1,0:T(8,128)(2,1)}, u32[]{:S(2)}) copy-start(bf16[1,1,17,256,256]{4,3,2,1,0:T(8,128)(2,1)} %own_hbm.1) | copy-start | bytes 6684676
  2.3 1.6 %copy-start.1 = (bf16[1,1,17,256,256]{4,3,2,1,0:T(8,128)(2,1)S(1)}, bf16[1,1,17,256,256]{4,3,2,1,0:T(8,128)(2,1)}, u32[]{:S(2)}) copy-start(bf16[1,1,17,256,256]{4,3,2,1,0:T(8,128)(2,1)} %hand_hbm.1) | copy-start | bytes 6684676
  3.9 0.9 %copy-start.2 = (bf16[1,1,256,256]{3,2,1,0:T(8,128)(2,1)S(1)}, bf16[1,1,256,256]{3,2,1,0:T(8,128)(2,1)}, u32[]{:S(2)}) copy-start(bf16[1,1,256,256]{3,2,1,0:T(8,128)(2,1)} %psi_hbm.1) | copy-start | bytes 393220
  4.8 0.7 copy-start.3

commit v2 on v1

v2 whole, which is shorter than its diff:
```python
import functools

import jax
import jax.numpy as jnp
from jax import lax
from jax.experimental import pallas as pl
from jax.experimental.pallas import tpu as pltpu
from jax.sharding import PartitionSpec as P

MESH = pl.DeviceIdType.MESH


def kernel(
    width, pieces,
    psi_hbm, own_hbm, hand_hbm, src_ref,
    out_ref, alpha_ref, scale_ref,
    env, whole, whole2, first_ref, part_ref, tail_ref, full_ref,
    load_sem, z_send, z_recv, psi_send, psi_recv, *relay_sems,
):
    early_sems, late_sems = relay_sems[:4], relay_sems[4:]
    channels = own_hbm.shape[2]
    block = psi_hbm.shape[2]
    sec = lax.axis_index("sec")
    me = lax.axis_index("blk")
    odd = lax.rem(sec, 2)
    partner = {"sec": sec + 1 - 2 * odd}
    core = lax.rem(me, 2)
    sibling = me + 1 - 2 * core
    peers = [lax.rem(me + k, width) for k in range(1, width)]
    across = [lax.rem(me + 2 * k, width) for k in range(1, width // 2)]
    behind = [lax.rem(me + width - 2 * k, width) for k in range(1, width // 2)]
    sib_behind = [lax.rem(sibling + width - 2 * k, width) for k in range(1, width // 2)]

    barrier = pltpu.get_barrier_semaphore()
    pl.semaphore_signal(barrier, inc=1, device_id=partner, device_id_type=MESH)
    for k in peers:
        pl.semaphore_signal(barrier, inc=1, device_id={"blk": k}, device_id_type=MESH)
    load_own = pltpu.make_async_copy(own_hbm.at[0, 0], env.at[0], load_sem.at[0])
    load_psi = pltpu.make_async_copy(psi_hbm.at[0, 0], whole.at[me], load_sem.at[1])
    load_own.start()
    load_psi.start()
    pl.semaphore_wait(barrier, width)

    def z_copy(c):
        return pltpu.make_async_remote_copy(
            src_ref=hand_hbm.at[0, 0, c], dst_ref=env.at[1, c],
            send_sem=z_send.at[c], recv_sem=z_recv.at[c],
            device_id=partner, device_id_type=MESH,
        )

    @pl.loop(0, channels)
    def _(c):
        z_copy(c).start()

    def psi_copy(k):
        return pltpu.make_async_remote_copy(
            src_ref=psi_hbm.at[0, 0], dst_ref=whole.at[me],
            send_sem=psi_send.at[k], recv_sem=psi_recv.at[k],
            device_id={"blk": peers[k]}, device_id_type=MESH,
        )

    for k in range(width - 1):
        psi_copy(k).start()
    load_own.wait()
    load_psi.wait()
    for k in range(width - 1):
        psi_copy(k).wait()

    def term(v, c):
        inner = jnp.dot(
            v[src_ref[0, 0, c]], env[1 - odd, c], preferred_element_type=jnp.float32
        ).astype(jnp.bfloat16)
        return jnp.dot(env[odd, c], inner, preferred_element_type=jnp.float32)

    rows = block // pieces
    hops = width // 2 - 1

    def relay(buf, sems):
        v_send, v_recv, f_send, f_recv = sems

        def direct(k, i):
            part = buf.at[me, pl.ds(i * rows, rows)]
            return pltpu.make_async_remote_copy(
                src_ref=part, dst_ref=part,
                send_sem=v_send.at[k + 1, i], recv_sem=v_recv.at[k + 1, i],
                device_id={"blk": sibling if k < 0 else across[k]}, device_id_type=MESH,
            )

        def passed(k, i):
            part = buf.at[behind[k], pl.ds(i * rows, rows)]
            return pltpu.make_async_remote_copy(
                src_ref=part, dst_ref=part,
                send_sem=f_send.at[k, i], recv_sem=f_recv.at[k, i],
                device_id={"blk": sibling}, device_id_type=MESH,
            )

        def start():
            for k in [*range(hops), -1]:
                for i in range(pieces):
                    direct(k, i).start()

        def forward():
            for k in range(hops):
                for i in range(pieces):
                    direct(k, i).wait_recv()
                    passed(k, i).start()

        def arrive():
            for i in range(pieces):
                direct(-1, i).wait_recv()
            for k in range(hops):
                for i in range(pieces):
                    passed(k, i).wait_recv()

        def drain():
            for i in range(pieces):
                for k in range(-1, hops):
                    direct(k, i).wait_send()
                for k in range(hops):
                    passed(k, i).wait_send()

        return start, forward, arrive, drain

    early = relay(part_ref, early_sems)
    late = relay(tail_ref, late_sems)

    def channels_from(lo, hi):
        first_ref[...] = jnp.zeros_like(first_ref)
        add_channels(lo, hi)

    def add_channels(lo, hi):
        @pl.loop(lo, hi)
        def _(c):
            z_copy(c).wait_recv()
            first_ref[...] += term(whole, c)

    cut = max(channels - 5, 0)
    channels_from(0, cut)
    part_ref[me] = first_ref[...]
    early[0]()
    channels_from(cut, cut + 3)
    early[1]()
    add_channels(cut + 3, channels - 1)
    early[2]()

    def fold(x):
        return jnp.sum(x.reshape(block // 8, 8, block), axis=0)

    mass = jnp.zeros((8, block), jnp.float32)
    for j in range(width):
        p = whole[j].astype(jnp.float32)
        mass += fold(p * p)
    mass = jnp.sum(mass, keepdims=True)
    add_channels(channels - 1, channels)
    tail_ref[me] = first_ref[...].astype(jnp.bfloat16)
    late[0]()
    early[3]()
    late[1]()
    late[2]()

    along = jnp.zeros((8, block), jnp.float32)
    for j in range(width):
        f = part_ref[j] + tail_ref[j].astype(jnp.float32)
        full_ref[j] = f
        along += fold(whole[j].astype(jnp.float32) * f)
    alpha = jnp.sum(along, keepdims=True) / mass
    power = jnp.zeros((8, block), jnp.float32)
    for j in range(width):
        rest = full_ref[j] - alpha * whole[j].astype(jnp.float32)
        full_ref[j] = rest
        power += fold(rest * rest)
    scale = jnp.sqrt(jnp.sum(power, keepdims=True) / (width * block * block) + 1e-06)
    factor = 1.0 / scale
    for j in range(width):
        whole2[j] = (full_ref[j] * factor).astype(jnp.bfloat16)

    total = term(whole2, 0)
    for c in range(1, channels):
        total += term(whole2, c)
    out_ref[0, 0] = total.astype(jnp.bfloat16)
    alpha_ref[0] = alpha[0, 0]
    scale_ref[0] = scale[0, 0]

    late[3]()

    @pl.loop(0, channels)
    def _(c):
        z_copy(c).wait_send()


def shards(width, psi, own_env, handoff_env, sources):
    channels = sources.shape[2]
    block = psi.shape[2]
    pieces = 2
    hops = width // 2 - 1
    dma = pltpu.SemaphoreType.DMA
    bf16, f32 = jnp.bfloat16, jnp.float32
    hbm = pl.BlockSpec(memory_space=pltpu.HBM)
    return pl.pallas_call(
        functools.partial(kernel, width, pieces),
        out_shape=(
            jax.ShapeDtypeStruct(psi.shape, bf16),
            jax.ShapeDtypeStruct((1,), f32),
            jax.ShapeDtypeStruct((1,), f32),
        ),
        in_specs=[hbm, hbm, hbm, pl.BlockSpec(memory_space=pltpu.SMEM)],
        out_specs=(
            pl.BlockSpec(memory_space=pltpu.VMEM),
            pl.BlockSpec(memory_space=pltpu.SMEM),
            pl.BlockSpec(memory_space=pltpu.SMEM),
        ),
        scratch_shapes=[
            pltpu.VMEM((2, channels, block, block), bf16),
            pltpu.VMEM((width, block, block), bf16),
            pltpu.VMEM((width, block, block), bf16),
            pltpu.VMEM((block, block), f32),
            pltpu.VMEM((width, block, block), f32),
            pltpu.VMEM((width, block, block), bf16),
            pltpu.VMEM((width, block, block), f32),
            dma((2,)),
            dma((channels,)), dma((channels,)),
            dma((width - 1,)), dma((width - 1,)),
            *[dma((n, pieces)) for n in (hops + 1, hops + 1, hops, hops) * 2],
        ],
        compiler_params=pltpu.CompilerParams(
            collective_id=0, has_side_effects=True, vmem_limit_bytes=62 * 2**20
        ),
        cost_estimate=pl.CostEstimate(
            flops=8 * channels * block**3, bytes_accessed=6 * channels * block**2,
            transcendentals=0,
        ),
    )(psi, own_env, handoff_env, sources)


def solution(mesh):
    in_specs = (
        P(("groups", "sec"), "blk", None, None),
        P(("groups", "sec"), "blk", None, None, None),
        P(("groups", "sec"), "blk", None, None, None),
        P(("groups", "sec"), "blk", None),
    )
    out_specs = (
        P(("groups", "sec"), "blk", None, None),
        P(("groups", "sec")),
        P(("groups", "sec")),
    )
    body = functools.partial(shards, mesh.shape["blk"])
    return jax.shard_map(body, mesh=mesh, in_specs=in_specs, out_specs=out_specs, check_vma=False)
```

time: 75.4 us -> 68.7 us (0.911)
  local copies, waits for them, and re-layouts: 5.46 us -> 1.57 us
  Pallas kernels: 65.7 us -> 62.8 us
    unnamed x9 -> x1, local copies, waits for them, and re-layouts: 5.46 us -> 1.57 us
    pallas_call x1, Pallas kernels: 65.7 us -> 62.8 us  [shards(): pl.pallas_call(functools.partial(kernel, width, pieces), out_shape=(jax.S...]
where the time goes in v2:
time: 68.7 us; the launch traced here: 68.5 us
  Pallas kernels  62.8 us (91%)
  between operations  4.2 us (6%)
  local copies, waits for them, and re-layouts  1.57 us (2%)
    pallas_call x1, Pallas kernels, shards(): pl.pallas_call(functools.partial(kernel, width, pieces), out_shape=(jax.S...  62.8 us
    unnamed x1, local copies, waits for them, and re-layouts  1.57 us

profile of v2, /device:TPU:1, one launch (start us, length us, event | category | flops | bytes accessed | tf_op | source)
XLA Modules:
  0.0 68.5 jit_solution(13512852524168207578)
XLA Ops:
  0.6 62.8 %shard_map.67 = (bf16[1,1,256,256]{3,2,1,0:T(8,128)(2,1)}, f32[1]{0:T(128)}, f32[1]{0:T(128)}) custom-call(bf16[1,1,256,256]{3,2,1,0:T(8,128)(2,1)} %psi_hbm.1, bf16[1,1,17,256,256]{4,3,2,1,0:T(8,128)(2,1)} %own_hbm.1, bf16[1,1,17,256,256]{4,3,2,1,0:T(8,128)(2,1)} %hand_hbm.1, s32[1,1,17]{2,1,0:T(1,128)} %src_ref.1), custom_call_target="tpu_custom_call" | custom-call | flops 2281701376 | bytes 6684672 | tf_op jit(solution)/shard_map/pallas_call | solution.py:199
  63.4 1.6 %copy.10 = bf16[1,1,256,256]{3,2,1,0:T(8,128)(2,1)} copy(bf16[1,1,256,256]{3,2,1,0:T(8,128)(2,1)} %get-tuple-element.6) | data formatting | bytes 262144

commit v3 on v2

--- a/solution.py
+++ b/solution.py
@@ -11,15 +11,15 @@
 
 
 def kernel(
-    width, pieces,
+    width,
     psi_hbm, own_hbm, hand_hbm, src_ref,
     out_ref, alpha_ref, scale_ref,
-    env, whole, whole2, first_ref, part_ref, tail_ref, full_ref,
+    env, whole, whole2, first_ref, part_ref, tail_ref, psi_ref,
     load_sem, z_send, z_recv, psi_send, psi_recv, *relay_sems,
 ):
-    early_sems, late_sems = relay_sems[:4], relay_sems[4:]
     channels = own_hbm.shape[2]
     block = psi_hbm.shape[2]
+    half = block // 2
     sec = lax.axis_index("sec")
     me = lax.axis_index("blk")
     odd = lax.rem(sec, 2)
@@ -41,16 +41,25 @@
     load_psi.start()
     pl.semaphore_wait(barrier, width)
 
-    def z_copy(c):
+    def z_copy(by_rows, h, c):
+        cut = (pl.ds(h * half, half), slice(None))
+        cut = cut if by_rows else cut[::-1]
         return pltpu.make_async_remote_copy(
-            src_ref=hand_hbm.at[0, 0, c], dst_ref=env.at[1, c],
-            send_sem=z_send.at[c], recv_sem=z_recv.at[c],
+            src_ref=hand_hbm.at[(0, 0, c, *cut)], dst_ref=env.at[(1, c, *cut)],
+            send_sem=z_send.at[h, c], recv_sem=z_recv.at[h, c],
             device_id=partner, device_id_type=MESH,
         )
 
-    @pl.loop(0, channels)
-    def _(c):
-        z_copy(c).start()
+    def outgoing(act):
+        for parity in range(2):
+            @pl.when(odd == parity)
+            def _():
+                for h in range(2):
+                    @pl.loop(0, channels)
+                    def _(c):
+                        act(z_copy(parity == 0, h, c))
+
+    outgoing(lambda copy: copy.start())
 
     def psi_copy(k):
         return pltpu.make_async_remote_copy(
@@ -72,14 +81,14 @@
         ).astype(jnp.bfloat16)
         return jnp.dot(env[odd, c], inner, preferred_element_type=jnp.float32)
 
-    rows = block // pieces
+    pieces = 2
     hops = width // 2 - 1
 
-    def relay(buf, sems):
+    def relay(buf, lo, sems):
         v_send, v_recv, f_send, f_recv = sems
 
         def direct(k, i):
-            part = buf.at[me, pl.ds(i * rows, rows)]
+            part = buf.at[me, lo + i]
             return pltpu.make_async_remote_copy(
                 src_ref=part, dst_ref=part,
                 send_sem=v_send.at[k + 1, i], recv_sem=v_recv.at[k + 1, i],
@@ -87,7 +96,7 @@
             )
 
         def passed(k, i):
-            part = buf.at[behind[k], pl.ds(i * rows, rows)]
+            part = buf.at[behind[k], lo + i]
             return pltpu.make_async_remote_copy(
                 src_ref=part, dst_ref=part,
                 send_sem=f_send.at[k, i], recv_sem=f_recv.at[k, i],
@@ -121,58 +130,93 @@
 
         return start, forward, arrive, drain
 
-    early = relay(part_ref, early_sems)
-    late = relay(tail_ref, late_sems)
-
-    def channels_from(lo, hi):
-        first_ref[...] = jnp.zeros_like(first_ref)
-        add_channels(lo, hi)
-
-    def add_channels(lo, hi):
-        @pl.loop(lo, hi)
-        def _(c):
-            z_copy(c).wait_recv()
-            first_ref[...] += term(whole, c)
-
-    cut = max(channels - 5, 0)
-    channels_from(0, cut)
-    part_ref[me] = first_ref[...]
-    early[0]()
-    channels_from(cut, cut + 3)
-    early[1]()
-    add_channels(cut + 3, channels - 1)
-    early[2]()
+    upper, lower = 2 - odd, 1 + odd
+    head = relay(part_ref, 0, relay_sems[:4])
+    early = relay(part_ref, 2, relay_sems[4:8])
+    late = relay(tail_ref, 0, relay_sems[8:])
+
+    def add_channels(h, lo, hi):
+        cut = pl.ds(h * half, half)
+
+        @pl.when(odd == 0)
+        def _():
+            @pl.loop(lo, hi)
+            def _(c):
+                z_copy(False, h, c).wait_recv()
+                inner = jnp.dot(
+                    whole[src_ref[0, 0, c]], env[1, c, :, cut], preferred_element_type=jnp.float32
+                ).astype(jnp.bfloat16)
+                x = jnp.dot(env[0, c], inner, preferred_element_type=jnp.float32)
+                first_ref[0] += x[:half]
+                first_ref[1] += x[half:]
+
+        @pl.when(odd == 1)
+        def _():
+            @pl.loop(lo, hi)
+            def _(c):
+                z_copy(True, h, c).wait_recv()
+                inner = jnp.dot(
+                    whole[src_ref[0, 0, c]], env[0, c], preferred_element_type=jnp.float32
+                ).astype(jnp.bfloat16)
+                x = jnp.dot(env[1, c, cut, :], inner, preferred_element_type=jnp.float32)
+                first_ref[0] += x[:, :half]
+                first_ref[1] += x[:, half:]
 
     def fold(x):
-        return jnp.sum(x.reshape(block // 8, 8, block), axis=0)
-
-    mass = jnp.zeros((8, block), jnp.float32)
-    for j in range(width):
-        p = whole[j].astype(jnp.float32)
+        return jnp.sum(x.reshape(-1, 8, half), axis=0)
+
+    cut = max(channels - 6, 0)
+    first_ref[...] = jnp.zeros_like(first_ref)
+    add_channels(0, 0, channels)
+    part_ref[me, 0:2] = first_ref[...]
+    head[0]()
+    first_ref[...] = jnp.zeros_like(first_ref)
+    mass = jnp.zeros((8, half), jnp.float32)
+    for j in range(width):
+        p = whole[j]
+        psi_ref[j, 0] = p[:half, :half]
+        psi_ref[j, 3] = p[half:, half:]
+        psi_ref[j, upper] = p[:half, half:]
+        psi_ref[j, lower] = p[half:, :half]
+        p = psi_ref[j].astype(jnp.float32)
         mass += fold(p * p)
     mass = jnp.sum(mass, keepdims=True)
-    add_channels(channels - 1, channels)
+    add_channels(1, 0, cut // 2)
+    head[1]()
+    add_channels(1, cut // 2, cut)
+    part_ref[me, 2:4] = first_ref[...]
+    first_ref[...] = jnp.zeros_like(first_ref)
+    early[0]()
+    head[2]()
+    head[3]()
+    add_channels(1, cut, channels - 3)
+    early[1]()
+    add_channels(1, channels - 3, channels - 1)
+    early[2]()
+    early[3]()
+    add_channels(1, channels - 1, channels)
     tail_ref[me] = first_ref[...].astype(jnp.bfloat16)
     late[0]()
-    early[3]()
     late[1]()
     late[2]()
 
-    along = jnp.zeros((8, block), jnp.float32)
-    for j in range(width):
-        f = part_ref[j] + tail_ref[j].astype(jnp.float32)
-        full_ref[j] = f
-        along += fold(whole[j].astype(jnp.float32) * f)
+    along = jnp.zeros((8, half), jnp.float32)
+    for j in range(width):
+        part_ref[j, 2:4] += tail_ref[j].astype(jnp.float32)
+        along += fold(psi_ref[j].astype(jnp.float32) * part_ref[j])
     alpha = jnp.sum(along, keepdims=True) / mass
-    power = jnp.zeros((8, block), jnp.float32)
-    for j in range(width):
-        rest = full_ref[j] - alpha * whole[j].astype(jnp.float32)
-        full_ref[j] = rest
+    power = jnp.zeros((8, half), jnp.float32)
+    for j in range(width):
+        rest = part_ref[j] - alpha * psi_ref[j].astype(jnp.float32)
+        part_ref[j] = rest
         power += fold(rest * rest)
     scale = jnp.sqrt(jnp.sum(power, keepdims=True) / (width * block * block) + 1e-06)
     factor = 1.0 / scale
     for j in range(width):
-        whole2[j] = (full_ref[j] * factor).astype(jnp.bfloat16)
+        whole2[j, :half, :half] = (part_ref[j, 0] * factor).astype(jnp.bfloat16)
+        whole2[j, :half, half:] = (part_ref[j, upper] * factor).astype(jnp.bfloat16)
+        whole2[j, half:, :half] = (part_ref[j, lower] * factor).astype(jnp.bfloat16)
+        whole2[j, half:, half:] = (part_ref[j, 3] * factor).astype(jnp.bfloat16)
 
     total = term(whole2, 0)
     for c in range(1, channels):
@@ -183,21 +227,19 @@
 
     late[3]()
 
-    @pl.loop(0, channels)
-    def _(c):
-        z_copy(c).wait_send()
+    outgoing(lambda copy: copy.wait_send())
 
 
 def shards(width, psi, own_env, handoff_env, sources):
     channels = sources.shape[2]
     block = psi.shape[2]
-    pieces = 2
+    half = block // 2
     hops = width // 2 - 1
     dma = pltpu.SemaphoreType.DMA
     bf16, f32 = jnp.bfloat16, jnp.float32
     hbm = pl.BlockSpec(memory_space=pltpu.HBM)
     return pl.pallas_call(
-        functools.partial(kernel, width, pieces),
+        functools.partial(kernel, width),
         out_shape=(
             jax.ShapeDtypeStruct(psi.shape, bf16),
             jax.ShapeDtypeStruct((1,), f32),
@@ -213,14 +255,14 @@
             pltpu.VMEM((2, channels, block, block), bf16),
             pltpu.VMEM((width, block, block), bf16),
             pltpu.VMEM((width, block, block), bf16),
-            pltpu.VMEM((block, block), f32),
-            pltpu.VMEM((width, block, block), f32),
-            pltpu.VMEM((width, block, block), bf16),
-            pltpu.VMEM((width, block, block), f32),
+            pltpu.VMEM((2, half, half), f32),
+            pltpu.VMEM((width, 4, half, half), f32),
+            pltpu.VMEM((width, 2, half, half), bf16),
+            pltpu.VMEM((width, 4, half, half), bf16),
             dma((2,)),
-            dma((channels,)), dma((channels,)),
+            dma((2, channels)), dma((2, channels)),
             dma((width - 1,)), dma((width - 1,)),
-            *[dma((n, pieces)) for n in (hops + 1, hops + 1, hops, hops) * 2],
+            *[dma((n, 2)) for n in (hops + 1, hops + 1, hops, hops) * 3],
         ],
         compiler_params=pltpu.CompilerParams(
             collective_id=0, has_side_effects=True, vmem_limit_bytes=62 * 2**20

time: 68.7 us -> 68.3 us (level)
  no operation moved by 1% of the time
where the time goes in v3:
time: 68.3 us; the launch traced here: 68.1 us
  Pallas kernels  62.3 us (91%)
  between operations  4.2 us (6%)
  local copies, waits for them, and re-layouts  1.57 us (2%)
    pallas_call x1, Pallas kernels, shards(): pl.pallas_call(functools.partial(kernel, width), out_shape=(jax.ShapeDtyp...  62.3 us
    unnamed x1, local copies, waits for them, and re-layouts  1.57 us

profile of v3, /device:TPU:1, one launch (start us, length us, event | category | flops | bytes accessed | tf_op | source)
XLA Modules:
  0.0 68.1 jit_solution(8983938683913131641)
XLA Ops:
  0.6 62.3 %shard_map.67 = (bf16[1,1,256,256]{3,2,1,0:T(8,128)(2,1)}, f32[1]{0:T(128)}, f32[1]{0:T(128)}) custom-call(bf16[1,1,256,256]{3,2,1,0:T(8,128)(2,1)} %psi_hbm.1, bf16[1,1,17,256,256]{4,3,2,1,0:T(8,128)(2,1)} %own_hbm.1, bf16[1,1,17,256,256]{4,3,2,1,0:T(8,128)(2,1)} %hand_hbm.1, s32[1,1,17]{2,1,0:T(1,128)} %src_ref.1), custom_call_target="tpu_custom_call" | custom-call | flops 2281701376 | bytes 6684672 | tf_op jit(solution)/shard_map/pallas_call | solution.py:241
  63.0 1.6 %copy.10 = bf16[1,1,256,256]{3,2,1,0:T(8,128)(2,1)} copy(bf16[1,1,256,256]{3,2,1,0:T(8,128)(2,1)} %get-tuple-element.6) | data formatting | bytes 262144

commit v4 on v3

--- a/solution.py
+++ b/solution.py
@@ -14,7 +14,7 @@
     width,
     psi_hbm, own_hbm, hand_hbm, src_ref,
     out_ref, alpha_ref, scale_ref,
-    env, whole, whole2, first_ref, part_ref, tail_ref, psi_ref,
+    env, whole, whole2, first_ref, part_ref, psi_ref, rest_ref,
     load_sem, z_send, z_recv, psi_send, psi_recv, *relay_sems,
 ):
     channels = own_hbm.shape[2]
@@ -132,8 +132,7 @@
 
     upper, lower = 2 - odd, 1 + odd
     head = relay(part_ref, 0, relay_sems[:4])
-    early = relay(part_ref, 2, relay_sems[4:8])
-    late = relay(tail_ref, 0, relay_sems[8:])
+    late = relay(part_ref, 2, relay_sems[4:])
 
     def add_channels(h, lo, hi):
         cut = pl.ds(h * half, half)
@@ -184,39 +183,31 @@
     add_channels(1, 0, cut // 2)
     head[1]()
     add_channels(1, cut // 2, cut)
-    part_ref[me, 2:4] = first_ref[...]
-    first_ref[...] = jnp.zeros_like(first_ref)
-    early[0]()
     head[2]()
     head[3]()
-    add_channels(1, cut, channels - 3)
-    early[1]()
-    add_channels(1, channels - 3, channels - 1)
-    early[2]()
-    early[3]()
+    add_channels(1, cut, channels - 1)
     add_channels(1, channels - 1, channels)
-    tail_ref[me] = first_ref[...].astype(jnp.bfloat16)
+    part_ref[me, 2:4] = first_ref[...]
     late[0]()
     late[1]()
     late[2]()
 
     along = jnp.zeros((8, half), jnp.float32)
     for j in range(width):
-        part_ref[j, 2:4] += tail_ref[j].astype(jnp.float32)
         along += fold(psi_ref[j].astype(jnp.float32) * part_ref[j])
     alpha = jnp.sum(along, keepdims=True) / mass
     power = jnp.zeros((8, half), jnp.float32)
     for j in range(width):
         rest = part_ref[j] - alpha * psi_ref[j].astype(jnp.float32)
-        part_ref[j] = rest
+        rest_ref[j] = rest
         power += fold(rest * rest)
     scale = jnp.sqrt(jnp.sum(power, keepdims=True) / (width * block * block) + 1e-06)
     factor = 1.0 / scale
     for j in range(width):
-        whole2[j, :half, :half] = (part_ref[j, 0] * factor).astype(jnp.bfloat16)
-        whole2[j, :half, half:] = (part_ref[j, upper] * factor).astype(jnp.bfloat16)
-        whole2[j, half:, :half] = (part_ref[j, lower] * factor).astype(jnp.bfloat16)
-        whole2[j, half:, half:] = (part_ref[j, 3] * factor).astype(jnp.bfloat16)
+        whole2[j, :half, :half] = (rest_ref[j, 0] * factor).astype(jnp.bfloat16)
+        whole2[j, :half, half:] = (rest_ref[j, upper] * factor).astype(jnp.bfloat16)
+        whole2[j, half:, :half] = (rest_ref[j, lower] * factor).astype(jnp.bfloat16)
+        whole2[j, half:, half:] = (rest_ref[j, 3] * factor).astype(jnp.bfloat16)
 
     total = term(whole2, 0)
     for c in range(1, channels):
@@ -257,12 +248,12 @@
             pltpu.VMEM((width, block, block), bf16),
             pltpu.VMEM((2, half, half), f32),
             pltpu.VMEM((width, 4, half, half), f32),
-            pltpu.VMEM((width, 2, half, half), bf16),
             pltpu.VMEM((width, 4, half, half), bf16),
+            pltpu.VMEM((width, 4, half, half), f32),
             dma((2,)),
             dma((2, channels)), dma((2, channels)),
             dma((width - 1,)), dma((width - 1,)),
-            *[dma((n, 2)) for n in (hops + 1, hops + 1, hops, hops) * 3],
+            *[dma((n, 2)) for n in (hops + 1, hops + 1, hops, hops) * 2],
         ],
         compiler_params=pltpu.CompilerParams(
             collective_id=0, has_side_effects=True, vmem_limit_bytes=62 * 2**20

time: 68.3 us -> 69.2 us (1.013)
  Pallas kernels: 62.3 us -> 63.3 us
    pallas_call x1, Pallas kernels: 62.3 us -> 63.3 us  [shards(): pl.pallas_call(functools.partial(kernel, width), out_shape=(jax.ShapeDtyp...]
where the time goes in v4:
time: 69.2 us; the launch traced here: 69 us
  Pallas kernels  63.3 us (91%)
  between operations  4.2 us (6%)
  local copies, waits for them, and re-layouts  1.57 us (2%)
    pallas_call x1, Pallas kernels, shards(): pl.pallas_call(functools.partial(kernel, width), out_shape=(jax.ShapeDtyp...  63.3 us
    unnamed x1, local copies, waits for them, and re-layouts  1.57 us

profile of v4, /device:TPU:1, one launch (start us, length us, event | category | flops | bytes accessed | tf_op | source)
XLA Modules:
  0.0 69.0 jit_solution(16780710211811962786)
XLA Ops:
  0.6 63.3 %shard_map.67 = (bf16[1,1,256,256]{3,2,1,0:T(8,128)(2,1)}, f32[1]{0:T(128)}, f32[1]{0:T(128)}) custom-call(bf16[1,1,256,256]{3,2,1,0:T(8,128)(2,1)} %psi_hbm.1, bf16[1,1,17,256,256]{4,3,2,1,0:T(8,128)(2,1)} %own_hbm.1, bf16[1,1,17,256,256]{4,3,2,1,0:T(8,128)(2,1)} %hand_hbm.1, s32[1,1,17]{2,1,0:T(1,128)} %src_ref.1), custom_call_target="tpu_custom_call" | custom-call | flops 2281701376 | bytes 6684672 | tf_op jit(solution)/shard_map/pallas_call | solution.py:232
  63.9 1.6 %copy.10 = bf16[1,1,256,256]{3,2,1,0:T(8,128)(2,1)} copy(bf16[1,1,256,256]{3,2,1,0:T(8,128)(2,1)} %get-tuple-element.6) | data formatting | bytes 262144
